TPU v7x, 256 devices: a whole 4x4x8 slice. The times are simulated.
256 devices in a mesh: dp: 128 (over z, x, y), pair: 2 (over core).
Axes of the slice: x: 4, y: 4, z: 8, core: 2. Of those that a mesh axis runs over, the one named last changes fastest.
Arguments:
- hidden_in: bfloat16 [32768, 1536], P(('dp', 'pair')), may hold values from -24 to 24
- segment_ids: int32 [32768], replicated, may hold values from 0 to 511, as said below
- frame_mask: int32 [32768], P(('dp', 'pair')), may hold values from 0 to 1, as said below
- dw_kernel: float32 [31, 1536], P(None, ('dp', 'pair')), may hold values from -1 to 1
- norm_scale: float32 [1536], P(('dp', 'pair')), may hold values from 0.1 to 1.9
- norm_shift: float32 [1536], P(('dp', 'pair')), may hold values from -3 to 3
- out_weight: bfloat16 [1536, 1536], P(('dp', 'pair')), may hold values from -0.15625 to 0.15625
- cotangent: bfloat16 [32768, 1536], P(('dp', 'pair')), may hold values from -6 to 6
Outputs:
- module_out: bfloat16 [32768, 1536], P(('dp', 'pair'))
- grad_hidden: bfloat16 [32768, 1536], P(('dp', 'pair'))
- grad_kernel: float32 [31, 1536], P(None, ('dp', 'pair'))
- grad_scale: float32 [1536], P(('dp', 'pair'))
- grad_shift: float32 [1536], P(('dp', 'pair'))
- grad_weight: float32 [1536, 1536], P(('dp', 'pair'))
Inputs may be any that keep to these rules, and one draw needn't show every extreme that they name: `segment_ids`: non-falling along the stream, starting at 0; each utterance has 1 to 192 frames; no utterance begins at a frame whose index is a positive multiple of 128. `frame_mask`: 1 on every frame whose index modulo 16 is 0 or 15.
All inputs are finite; a program needn't handle non-finite values.
Results may differ from a plain program's by a relative error of at most 0.0049.
Values may be sent and summed in bfloat16 or wider, within the bound.
No kernel may reach another device: no remote copies, remote signals or barrier semaphores. Data moves between devices by JAX's collectives and lax.ppermute only.
A program may use at most 128 MiB of HBM per device.

v0:
```python
import jax
import jax.numpy as jnp
from jax import lax
from jax.sharding import PartitionSpec as P

KERNEL = 31


def padded(cells, sides, width):
    for axis, dim in sides:
        count = lax.axis_size(axis)
        ends = count - 1
        head = lax.slice_in_dim(cells, 0, width, axis=dim)
        tail = lax.slice_in_dim(cells, cells.shape[dim] - width, cells.shape[dim], axis=dim)
        cells = jnp.concatenate(
            [
                lax.ppermute(tail, axis, [(i, (i + 1) % count) for i in range(ends)]),
                cells,
                lax.ppermute(head, axis, [((i + 1) % count, i) for i in range(ends)]),
            ],
            axis=dim,
        )
    return cells


def local(
    hidden_in, segment_ids, frame_mask, dw_kernel, norm_scale, norm_shift, out_weight, cotangent
):
    local_rows = hidden_in.shape[0]
    shard_cols = norm_scale.shape[0]
    half = KERNEL // 2
    device_pos = lax.axis_index(("dp", "pair"))
    weight_col = frame_mask.astype(jnp.float32)[:, None]
    stacked = jnp.concatenate([dw_kernel, norm_scale[None, :], norm_shift[None, :]], axis=0)
    params_full = lax.all_gather(stacked, ("dp", "pair"), axis=1, tiled=True)
    kernel_full = params_full[:KERNEL]
    scale_full = params_full[KERNEL]
    shift_full = params_full[KERNEL + 1]
    seg_pad = jnp.pad(segment_ids, (half, half), constant_values=-1)
    seg_local = lax.dynamic_slice_in_dim(seg_pad, device_pos * local_rows, local_rows + 2 * half)
    own_seg = seg_local[half : half + local_rows]
    masked = jnp.where(frame_mask[:, None] == 1, hidden_in, jnp.zeros_like(hidden_in))
    padded_in = padded(masked, ((("dp", "pair"), 0),), half).astype(jnp.float32)
    conv = jnp.zeros((local_rows, params_full.shape[1]), jnp.float32)
    for offset in range(KERNEL):
        same_seg = (seg_local[offset : offset + local_rows] == own_seg)[:, None]
        conv = conv + jnp.where(
            same_seg, kernel_full[offset] * padded_in[offset : offset + local_rows], 0.0
        )
    total, count = lax.psum(
        (jnp.sum(weight_col * conv, axis=0), jnp.sum(weight_col)), ("dp", "pair")
    )
    mean = total / count
    centred = conv - mean
    spread = lax.psum(jnp.sum(weight_col * centred * centred, axis=0), ("dp", "pair"))
    variance = spread / count
    inv_std = lax.rsqrt(variance + 1e-05)
    normed = centred * inv_std
    pre = scale_full * normed + shift_full
    sig = jax.nn.sigmoid(pre)
    act = (weight_col * pre * sig).astype(jnp.bfloat16)
    weight_full = lax.all_gather(out_weight, ("dp", "pair"), axis=0, tiled=True)
    module_out = jnp.dot(act, weight_full, preferred_element_type=jnp.float32).astype(jnp.bfloat16)
    grad_act = lax.dot_general(
        cotangent, weight_full, (((1,), (1,)), ((), ())), preferred_element_type=jnp.float32
    )
    grad_pre = weight_col * grad_act * sig * (1.0 + pre * (1.0 - sig))
    scale_sum, shift_sum = lax.psum(
        (jnp.sum(grad_pre * normed, axis=0), jnp.sum(grad_pre, axis=0)), ("dp", "pair")
    )
    col_start = device_pos * shard_cols
    grad_scale = lax.dynamic_slice_in_dim(scale_sum, col_start, shard_cols)
    grad_shift = lax.dynamic_slice_in_dim(shift_sum, col_start, shard_cols)
    grad_conv = (
        weight_col
        * scale_full
        * inv_std
        * (grad_pre - shift_sum / count - normed * scale_sum / count)
    )
    grad_pad = padded(grad_conv, ((("dp", "pair"), 0),), half)
    grad_local = jnp.zeros_like(grad_conv)
    tap_rows = []
    for offset in range(KERNEL):
        same_fwd = (seg_local[offset : offset + local_rows] == own_seg)[:, None]
        tap_rows.append(
            jnp.sum(
                jnp.where(same_fwd, grad_conv * padded_in[offset : offset + local_rows], 0.0),
                axis=0,
            )
        )
        back = 2 * half - offset
        same_back = (seg_local[back : back + local_rows] == own_seg)[:, None]
        grad_local = grad_local + jnp.where(
            same_back, kernel_full[offset] * grad_pad[back : back + local_rows], 0.0
        )
    grad_kernel = lax.psum_scatter(
        jnp.stack(tap_rows, axis=0), ("dp", "pair"), scatter_dimension=1, tiled=True
    )
    grad_hidden = (weight_col * grad_local).astype(jnp.bfloat16)
    grad_weight = lax.psum_scatter(
        lax.dot_general(
            act, cotangent, (((0,), (0,)), ((), ())), preferred_element_type=jnp.float32
        ),
        ("dp", "pair"),
        scatter_dimension=0,
        tiled=True,
    )
    return (module_out, grad_hidden, grad_kernel, grad_scale, grad_shift, grad_weight)


def solution(mesh):
    return jax.shard_map(
        local,
        mesh=mesh,
        in_specs=(
            P(("dp", "pair"), None),
            P(),
            P(("dp", "pair")),
            P(None, ("dp", "pair")),
            P(("dp", "pair")),
            P(("dp", "pair")),
            P(("dp", "pair"), None),
            P(("dp", "pair"), None),
        ),
        out_specs=(
            P(("dp", "pair"), None),
            P(("dp", "pair"), None),
            P(None, ("dp", "pair")),
            P(("dp", "pair")),
            P(("dp", "pair")),
            P(("dp", "pair"), None),
        ),
        check_vma=False,
    )
```

profile of v0, /device:TPU:1, one launch (start us, length us, event | category | flops | bytes accessed | tf_op | source)
XLA Modules:
  0.0 1933.7 jit_solution(4667449494425731221)
XLA Ops:
  9.7 4.6 collective-permute-start
  14.3 1.9 collective-permute-start.1
  19.3 68.0 %all-gather = f32[256,6,33]{2,1,0:T(8,128)S(1)} all-gather(f32[1,6,33]{2,1,0:T(8,128)S(1)} %maximum_bitcast_fusion), channel_id=1, replica_groups=mesh['dp'=128,'pair'=2] {'dp','pair'}, dimensions={0}, use_global_device_ids=true | all-gather | bytes 203544 | tf_op jit(solution)/shard_map/all_gather | solution.py:35
  88.0 5.6 slice_reduce_fusion.31
  93.6 8.2 slice_reduce_fusion.32
  102.8 4.6 multiply_reduce_fusion.2
  107.4 75.7 %all-reduce.5 = (f32[1536]{0:T(1024)S(1)}, f32[]{:T(128)}) all-reduce(f32[1536]{0:T(1024)S(1)} %get-tuple-element.89, f32[]{:T(128)} %convert_reduce_fusion), channel_id=1, replica_groups=mesh['dp'=128,'pair'=2] {'dp','pair'}, use_global_device_ids=true, to_apply=%region_1.2 | all-reduce | flops 1537 | bytes 12296 | tf_op jit(solution)/shard_map/psum | solution.py:50
  184.0 74.2 %psum.37 = f32[1536]{0:T(1024)S(1)} all-reduce(f32[1536]{0:T(1024)S(1)} %fusion.119), channel_id=1, replica_groups=mesh['dp'=128,'pair'=2] {'dp','pair'}, use_global_device_ids=true, to_apply=%region_5.6 | all-reduce | flops 1536 | bytes 12288 | tf_op jit(solution)/shard_map/psum | solution.py:55
  258.9 5.2 fusion.124
  264.0 709.9 %fusion = f32[8,1536]{1,0:T(8,128)S(1)} fusion(f32[1536,1536]{1,0:T(8,128)} %fusion.124), kind=kCustom, calls=%all-reduce-scatter | all-reduce-scatter fusion | flops 3145729 | bytes 9486336
  975.3 2.2 collective-permute-start.65
  978.8 11.0 collective-permute-start.67
  1005.7 17.9 collective-permute-start.51
  1023.7 3.1 collective-permute-start.50
  1028.4 2.8 collective-permute-start.48
  1031.3 3.9 collective-permute-start.47
  1035.2 3.9 collective-permute-start.46
  1045.8 2.8 collective-permute-start.40
  1048.6 3.6 collective-permute-start.39
  1052.3 2.5 collective-permute-start.38
  1054.7 4.1 collective-permute-start.37
  1060.5 6.1 collective-permute-start.35
  1066.6 13.1 collective-permute-start.34
  1079.7 13.1 collective-permute-start.33
  1092.9 13.1 collective-permute-start.32
  1106.0 13.1 collective-permute-start.31
  1119.2 13.1 collective-permute-start.30
  1132.3 13.1 collective-permute-start.29
  1145.5 13.1 collective-permute-start.28
  1158.6 13.1 collective-permute-start.27
  1171.8 13.1 collective-permute-start.26
  1184.9 13.1 collective-permute-start.25
  1198.1 13.1 collective-permute-start.24
  1211.2 13.1 collective-permute-start.23
  1224.4 13.1 collective-permute-start.22
  1237.5 13.1 collective-permute-start.21
  1250.7 13.1 collective-permute-start.20
  1263.8 13.1 collective-permute-start.19
  1277.0 13.1 collective-permute-start.18
  1290.1 13.1 collective-permute-start.17
  1303.3 13.1 collective-permute-start.16
  1316.4 13.3 collective-permute-start.15
  1329.7 13.1 collective-permute-start.14
  1342.9 13.1 collective-permute-start.13
  1356.0 13.1 collective-permute-start.12
  1369.2 13.1 collective-permute-start.11
  1382.3 13.1 collective-permute-start.10
  1395.5 13.1 collective-permute-start.9
  1408.6 13.7 collective-permute-start.8
  1422.4 13.1 collective-permute-start.7
  1435.5 13.1 collective-permute-start.6
  1448.7 13.1 collective-permute-start.5
  1461.8 3.0 collective-permute-start.4
  1466.0 97.2 %concatenate.45 = f32[518,1536]{1,0:T(8,128)} concatenate(f32[6,1536]{1,0:T(8,128)S(1)} %collective-permute-done.67, f32[8,1536]{1,0:T(8,128)S(1)} %collective-permute-done.66, f32[8,1536]{1,0:T(8,128)S(1)} %collective-permute-done.65, f32[8,1536]{1,0:T(8,128)S(1)} %collective-permute-done.64, f32[8,1536]{1,0:T(8,128)S(1)} %collective-permute-done.63, ...), dimensions={0} | concatenate | bytes 6365184
  1564.7 8.4 reshape.52
  1573.1 4.1 convolution_convert_fusion
  1577.3 2.6 fusion.125
  1580.0 79.5 %all-reduce.4 = (f32[1536]{0:T(1024)S(1)}, f32[1536]{0:T(1024)S(1)}) all-reduce(f32[1536]{0:T(1024)S(1)} %get-tuple-element.50, f32[1536]{0:T(1024)S(1)} %get-tuple-element.49), channel_id=1, replica_groups=mesh['dp'=128,'pair'=2] {'dp','pair'}, use_global_device_ids=true, to_apply=%region_9.10 | all-reduce | flops 3072 | bytes 24576 | tf_op jit(solution)/shard_map/psum | solution.py:68
  1660.3 3.5 select_reduce_fusion
  1667.3 2.6 collective-permute-start.2
  1669.9 3.2 collective-permute-start.3
  1675.3 2.7 stack.127
  1678.1 9.9 fusion.9
  1688.0 237.1 %all-reduce.8.cloned.1.call-done = f32[31,1536]{1,0:T(8,128)} async-done(((f32[31,1536]{1,0:T(8,128)}), f32[31,1536]{1,0:T(8,128)}) %all-reduce.8.cloned.1.call-update) | async-done | bytes 190480
  (330 shorter events, 46.3 us)
Async XLA Ops:
  7.2 1557.6 %all-gather.4.cloned.1.call-start = ((), (), s32[]{:S(2)}) async-start(), calls=%async_computation | async-start | bytes 6316032 | tf_op jit(solution)/shard_map/all_gather | solution.py:62
  7.9 1917.2 %all-reduce.8.cloned.1.call-start = ((), (), s32[]{:S(2)}) async-start(), calls=%async_computation.1 | async-start | bytes 393216
  9.7 92.7 %collective-permute-start = (bf16[15,1536]{1,0:T(8,128)(2,1)S(1)}, bf16[15,1536]{1,0:T(8,128)(2,1)S(1)}, u32[]{:S(2)}, u32[]{:S(2)}) collective-permute-start(bf16[15,1536]{1,0:T(8,128)(2,1)S(1)} %get-tuple-element.93), channel_id=1, source_target_pairs={{0,1},{1,2},{2,3},{3,4},{4,5},{5,6},{6,7},{7,8},{8,9},{9,10},{10,1... | collective-permute-start | bytes 138248 | tf_op jit(solution)/shard_map/ppermute | solution.py:17
  14.3 88.1 %collective-permute-start.1 = (bf16[15,1536]{1,0:T(8,128)(2,1)S(1)}, bf16[15,1536]{1,0:T(8,128)(2,1)S(1)}, u32[]{:S(2)}, u32[]{:S(2)}) collective-permute-start(bf16[15,1536]{1,0:T(8,128)(2,1)S(1)} %get-tuple-element.94), channel_id=1, source_target_pairs={{1,0},{2,1},{3,2},{4,3},{5,4},{6,5},{7,6},{8,7},{9,8},{10,9},{11,1... | collective-permute-start | bytes 138248 | tf_op jit(solution)/shard_map/ppermute | solution.py:19
  974.0 18.7 collective-permute-start.66
  975.3 18.7 collective-permute-start.65
  977.5 17.8 collective-permute-start.64
  978.8 12.5 collective-permute-start.67
  989.8 6.8 collective-permute-start.63
  992.6 6.5 collective-permute-start.61
  993.9 6.5 collective-permute-start.60
  1000.5 23.2 %collective-permute-start.55 = (f32[8,1536]{1,0:T(8,128)S(1)}, f32[8,1536]{1,0:T(8,128)S(1)}, u32[]{:S(2)}, u32[]{:S(2)}) collective-permute-start(f32[8,1536]{1,0:T(8,128)S(1)} %fusion), channel_id=1, source_target_pairs={{0,52},{1,53},{2,54},{3,55},{4,56},{5,57},{6,58},{7,59},{8,60},{9,... | collective-permute-start | bytes 147464
  1001.8 25.0 %collective-permute-start.54 = (f32[8,1536]{1,0:T(8,128)S(1)}, f32[8,1536]{1,0:T(8,128)S(1)}, u32[]{:S(2)}, u32[]{:S(2)}) collective-permute-start(f32[8,1536]{1,0:T(8,128)S(1)} %fusion), channel_id=1, source_target_pairs={{0,51},{1,52},{2,53},{3,54},{4,55},{5,56},{6,57},{7,58},{8,59},{9,... | collective-permute-start | bytes 147464
  1003.1 25.3 %collective-permute-start.53 = (f32[8,1536]{1,0:T(8,128)S(1)}, f32[8,1536]{1,0:T(8,128)S(1)}, u32[]{:S(2)}, u32[]{:S(2)}) collective-permute-start(f32[8,1536]{1,0:T(8,128)S(1)} %fusion), channel_id=1, source_target_pairs={{0,50},{1,51},{2,52},{3,53},{4,54},{5,55},{6,56},{7,57},{8,58},{9,... | collective-permute-start | bytes 147464
  1004.4 26.9 %collective-permute-start.52 = (f32[8,1536]{1,0:T(8,128)S(1)}, f32[8,1536]{1,0:T(8,128)S(1)}, u32[]{:S(2)}, u32[]{:S(2)}) collective-permute-start(f32[8,1536]{1,0:T(8,128)S(1)} %fusion), channel_id=1, source_target_pairs={{0,49},{1,50},{2,51},{3,52},{4,53},{5,54},{6,55},{7,56},{8,57},{9,... | collective-permute-start | bytes 147464
  1005.7 29.5 %collective-permute-start.51 = (f32[8,1536]{1,0:T(8,128)S(1)}, f32[8,1536]{1,0:T(8,128)S(1)}, u32[]{:S(2)}, u32[]{:S(2)}) collective-permute-start(f32[8,1536]{1,0:T(8,128)S(1)} %fusion), channel_id=1, source_target_pairs={{0,48},{1,49},{2,50},{3,51},{4,52},{5,53},{6,54},{7,55},{8,56},{9,... | collective-permute-start | bytes 147464
  1023.7 15.5 collective-permute-start.50
  1026.8 13.7 collective-permute-start.49
  1028.4 13.4 collective-permute-start.48
  1031.3 11.8 collective-permute-start.47
  1035.2 9.2 collective-permute-start.46
  1039.2 6.6 collective-permute-start.45
  1040.5 8.1 collective-permute-start.44
  1041.8 10.4 collective-permute-start.43
  1043.1 11.6 collective-permute-start.42
  1044.5 14.4 collective-permute-start.41
  1045.8 14.7 collective-permute-start.40
  1048.6 18.0 collective-permute-start.39
  1052.3 27.5 %collective-permute-start.38 = (f32[8,1536]{1,0:T(8,128)S(1)}, f32[8,1536]{1,0:T(8,128)S(1)}, u32[]{:S(2)}, u32[]{:S(2)}) collective-permute-start(f32[8,1536]{1,0:T(8,128)S(1)} %fusion), channel_id=1, source_target_pairs={{0,35},{1,36},{2,37},{3,38},{4,39},{5,40},{6,41},{7,42},{8,43},{9,... | collective-permute-start | bytes 147464
  1054.7 38.1 %collective-permute-start.37 = (f32[8,1536]{1,0:T(8,128)S(1)}, f32[8,1536]{1,0:T(8,128)S(1)}, u32[]{:S(2)}, u32[]{:S(2)}) collective-permute-start(f32[8,1536]{1,0:T(8,128)S(1)} %fusion), channel_id=1, source_target_pairs={{0,34},{1,35},{2,36},{3,37},{4,38},{5,39},{6,40},{7,41},{8,42},{9,... | collective-permute-start | bytes 147464
  1058.9 47.2 %collective-permute-start.36 = (f32[8,1536]{1,0:T(8,128)S(1)}, f32[8,1536]{1,0:T(8,128)S(1)}, u32[]{:S(2)}, u32[]{:S(2)}) collective-permute-start(f32[8,1536]{1,0:T(8,128)S(1)} %fusion), channel_id=1, source_target_pairs={{0,33},{1,34},{2,35},{3,36},{4,37},{5,38},{6,39},{7,40},{8,41},{9,... | collective-permute-start | bytes 147464
  1060.5 58.7 %collective-permute-start.35 = (f32[8,1536]{1,0:T(8,128)S(1)}, f32[8,1536]{1,0:T(8,128)S(1)}, u32[]{:S(2)}, u32[]{:S(2)}) collective-permute-start(f32[8,1536]{1,0:T(8,128)S(1)} %fusion), channel_id=1, source_target_pairs={{0,32},{1,33},{2,34},{3,35},{4,36},{5,37},{6,38},{7,39},{8,40},{9,... | collective-permute-start | bytes 147464
  1066.6 65.7 %collective-permute-start.34 = (f32[8,1536]{1,0:T(8,128)S(1)}, f32[8,1536]{1,0:T(8,128)S(1)}, u32[]{:S(2)}, u32[]{:S(2)}) collective-permute-start(f32[8,1536]{1,0:T(8,128)S(1)} %fusion), channel_id=1, source_target_pairs={{0,31},{1,32},{2,33},{3,34},{4,35},{5,36},{6,37},{7,38},{8,39},{9,... | collective-permute-start | bytes 147464
  1079.7 65.7 %collective-permute-start.33 = (f32[8,1536]{1,0:T(8,128)S(1)}, f32[8,1536]{1,0:T(8,128)S(1)}, u32[]{:S(2)}, u32[]{:S(2)}) collective-permute-start(f32[8,1536]{1,0:T(8,128)S(1)} %fusion), channel_id=1, source_target_pairs={{0,30},{1,31},{2,32},{3,33},{4,34},{5,35},{6,36},{7,37},{8,38},{9,... | collective-permute-start | bytes 147464
  1092.9 65.7 %collective-permute-start.32 = (f32[8,1536]{1,0:T(8,128)S(1)}, f32[8,1536]{1,0:T(8,128)S(1)}, u32[]{:S(2)}, u32[]{:S(2)}) collective-permute-start(f32[8,1536]{1,0:T(8,128)S(1)} %fusion), channel_id=1, source_target_pairs={{0,29},{1,30},{2,31},{3,32},{4,33},{5,34},{6,35},{7,36},{8,37},{9,... | collective-permute-start | bytes 147464
  1106.0 65.7 %collective-permute-start.31 = (f32[8,1536]{1,0:T(8,128)S(1)}, f32[8,1536]{1,0:T(8,128)S(1)}, u32[]{:S(2)}, u32[]{:S(2)}) collective-permute-start(f32[8,1536]{1,0:T(8,128)S(1)} %fusion), channel_id=1, source_target_pairs={{0,28},{1,29},{2,30},{3,31},{4,32},{5,33},{6,34},{7,35},{8,36},{9,... | collective-permute-start | bytes 147464
  1119.2 65.7 %collective-permute-start.30 = (f32[8,1536]{1,0:T(8,128)S(1)}, f32[8,1536]{1,0:T(8,128)S(1)}, u32[]{:S(2)}, u32[]{:S(2)}) collective-permute-start(f32[8,1536]{1,0:T(8,128)S(1)} %fusion), channel_id=1, source_target_pairs={{0,27},{1,28},{2,29},{3,30},{4,31},{5,32},{6,33},{7,34},{8,35},{9,... | collective-permute-start | bytes 147464
  1132.3 65.7 %collective-permute-start.29 = (f32[8,1536]{1,0:T(8,128)S(1)}, f32[8,1536]{1,0:T(8,128)S(1)}, u32[]{:S(2)}, u32[]{:S(2)}) collective-permute-start(f32[8,1536]{1,0:T(8,128)S(1)} %fusion), channel_id=1, source_target_pairs={{0,26},{1,27},{2,28},{3,29},{4,30},{5,31},{6,32},{7,33},{8,34},{9,... | collective-permute-start | bytes 147464
  1145.5 65.7 %collective-permute-start.28 = (f32[8,1536]{1,0:T(8,128)S(1)}, f32[8,1536]{1,0:T(8,128)S(1)}, u32[]{:S(2)}, u32[]{:S(2)}) collective-permute-start(f32[8,1536]{1,0:T(8,128)S(1)} %fusion), channel_id=1, source_target_pairs={{0,25},{1,26},{2,27},{3,28},{4,29},{5,30},{6,31},{7,32},{8,33},{9,... | collective-permute-start | bytes 147464
  1158.6 65.7 %collective-permute-start.27 = (f32[8,1536]{1,0:T(8,128)S(1)}, f32[8,1536]{1,0:T(8,128)S(1)}, u32[]{:S(2)}, u32[]{:S(2)}) collective-permute-start(f32[8,1536]{1,0:T(8,128)S(1)} %fusion), channel_id=1, source_target_pairs={{0,24},{1,25},{2,26},{3,27},{4,28},{5,29},{6,30},{7,31},{8,32},{9,... | collective-permute-start | bytes 147464
  1171.8 65.7 %collective-permute-start.26 = (f32[8,1536]{1,0:T(8,128)S(1)}, f32[8,1536]{1,0:T(8,128)S(1)}, u32[]{:S(2)}, u32[]{:S(2)}) collective-permute-start(f32[8,1536]{1,0:T(8,128)S(1)} %fusion), channel_id=1, source_target_pairs={{0,23},{1,24},{2,25},{3,26},{4,27},{5,28},{6,29},{7,30},{8,31},{9,... | collective-permute-start | bytes 147464
  1184.9 65.7 %collective-permute-start.25 = (f32[8,1536]{1,0:T(8,128)S(1)}, f32[8,1536]{1,0:T(8,128)S(1)}, u32[]{:S(2)}, u32[]{:S(2)}) collective-permute-start(f32[8,1536]{1,0:T(8,128)S(1)} %fusion), channel_id=1, source_target_pairs={{0,22},{1,23},{2,24},{3,25},{4,26},{5,27},{6,28},{7,29},{8,30},{9,... | collective-permute-start | bytes 147464
  1198.1 65.7 %collective-permute-start.24 = (f32[8,1536]{1,0:T(8,128)S(1)}, f32[8,1536]{1,0:T(8,128)S(1)}, u32[]{:S(2)}, u32[]{:S(2)}) collective-permute-start(f32[8,1536]{1,0:T(8,128)S(1)} %fusion), channel_id=1, source_target_pairs={{0,21},{1,22},{2,23},{3,24},{4,25},{5,26},{6,27},{7,28},{8,29},{9,... | collective-permute-start | bytes 147464
  1211.2 65.7 %collective-permute-start.23 = (f32[8,1536]{1,0:T(8,128)S(1)}, f32[8,1536]{1,0:T(8,128)S(1)}, u32[]{:S(2)}, u32[]{:S(2)}) collective-permute-start(f32[8,1536]{1,0:T(8,128)S(1)} %fusion), channel_id=1, source_target_pairs={{0,20},{1,21},{2,22},{3,23},{4,24},{5,25},{6,26},{7,27},{8,28},{9,... | collective-permute-start | bytes 147464
  1224.4 65.7 %collective-permute-start.22 = (f32[8,1536]{1,0:T(8,128)S(1)}, f32[8,1536]{1,0:T(8,128)S(1)}, u32[]{:S(2)}, u32[]{:S(2)}) collective-permute-start(f32[8,1536]{1,0:T(8,128)S(1)} %fusion), channel_id=1, source_target_pairs={{0,19},{1,20},{2,21},{3,22},{4,23},{5,24},{6,25},{7,26},{8,27},{9,... | collective-permute-start | bytes 147464
  1237.5 65.7 %collective-permute-start.21 = (f32[8,1536]{1,0:T(8,128)S(1)}, f32[8,1536]{1,0:T(8,128)S(1)}, u32[]{:S(2)}, u32[]{:S(2)}) collective-permute-start(f32[8,1536]{1,0:T(8,128)S(1)} %fusion), channel_id=1, source_target_pairs={{0,18},{1,19},{2,20},{3,21},{4,22},{5,23},{6,24},{7,25},{8,26},{9,... | collective-permute-start | bytes 147464
  1250.7 65.7 %collective-permute-start.20 = (f32[8,1536]{1,0:T(8,128)S(1)}, f32[8,1536]{1,0:T(8,128)S(1)}, u32[]{:S(2)}, u32[]{:S(2)}) collective-permute-start(f32[8,1536]{1,0:T(8,128)S(1)} %fusion), channel_id=1, source_target_pairs={{0,17},{1,18},{2,19},{3,20},{4,21},{5,22},{6,23},{7,24},{8,25},{9,... | collective-permute-start | bytes 147464
  1263.8 65.9 %collective-permute-start.19 = (f32[8,1536]{1,0:T(8,128)S(1)}, f32[8,1536]{1,0:T(8,128)S(1)}, u32[]{:S(2)}, u32[]{:S(2)}) collective-permute-start(f32[8,1536]{1,0:T(8,128)S(1)} %fusion), channel_id=1, source_target_pairs={{0,16},{1,17},{2,18},{3,19},{4,20},{5,21},{6,22},{7,23},{8,24},{9,... | collective-permute-start | bytes 147464
  1277.0 65.9 %collective-permute-start.18 = (f32[8,1536]{1,0:T(8,128)S(1)}, f32[8,1536]{1,0:T(8,128)S(1)}, u32[]{:S(2)}, u32[]{:S(2)}) collective-permute-start(f32[8,1536]{1,0:T(8,128)S(1)} %fusion), channel_id=1, source_target_pairs={{0,15},{1,16},{2,17},{3,18},{4,19},{5,20},{6,21},{7,22},{8,23},{9,... | collective-permute-start | bytes 147464
  1290.1 65.9 %collective-permute-start.17 = (f32[8,1536]{1,0:T(8,128)S(1)}, f32[8,1536]{1,0:T(8,128)S(1)}, u32[]{:S(2)}, u32[]{:S(2)}) collective-permute-start(f32[8,1536]{1,0:T(8,128)S(1)} %fusion), channel_id=1, source_target_pairs={{0,14},{1,15},{2,16},{3,17},{4,18},{5,19},{6,20},{7,21},{8,22},{9,... | collective-permute-start | bytes 147464
  1303.3 65.9 %collective-permute-start.16 = (f32[8,1536]{1,0:T(8,128)S(1)}, f32[8,1536]{1,0:T(8,128)S(1)}, u32[]{:S(2)}, u32[]{:S(2)}) collective-permute-start(f32[8,1536]{1,0:T(8,128)S(1)} %fusion), channel_id=1, source_target_pairs={{0,13},{1,14},{2,15},{3,16},{4,17},{5,18},{6,19},{7,20},{8,21},{9,... | collective-permute-start | bytes 147464
  1316.4 65.9 %collective-permute-start.15 = (f32[8,1536]{1,0:T(8,128)S(1)}, f32[8,1536]{1,0:T(8,128)S(1)}, u32[]{:S(2)}, u32[]{:S(2)}) collective-permute-start(f32[8,1536]{1,0:T(8,128)S(1)} %fusion), channel_id=1, source_target_pairs={{0,12},{1,13},{2,14},{3,15},{4,16},{5,17},{6,18},{7,19},{8,20},{9,... | collective-permute-start | bytes 147464
  1329.7 65.7 %collective-permute-start.14 = (f32[8,1536]{1,0:T(8,128)S(1)}, f32[8,1536]{1,0:T(8,128)S(1)}, u32[]{:S(2)}, u32[]{:S(2)}) collective-permute-start(f32[8,1536]{1,0:T(8,128)S(1)} %fusion), channel_id=1, source_target_pairs={{0,11},{1,12},{2,13},{3,14},{4,15},{5,16},{6,17},{7,18},{8,19},{9,... | collective-permute-start | bytes 147464
  1342.9 65.7 %collective-permute-start.13 = (f32[8,1536]{1,0:T(8,128)S(1)}, f32[8,1536]{1,0:T(8,128)S(1)}, u32[]{:S(2)}, u32[]{:S(2)}) collective-permute-start(f32[8,1536]{1,0:T(8,128)S(1)} %fusion), channel_id=1, source_target_pairs={{0,10},{1,11},{2,12},{3,13},{4,14},{5,15},{6,16},{7,17},{8,18},{9,... | collective-permute-start | bytes 147464
  1356.0 66.3 %collective-permute-start.12 = (f32[8,1536]{1,0:T(8,128)S(1)}, f32[8,1536]{1,0:T(8,128)S(1)}, u32[]{:S(2)}, u32[]{:S(2)}) collective-permute-start(f32[8,1536]{1,0:T(8,128)S(1)} %fusion), channel_id=1, source_target_pairs={{0,9},{1,10},{2,11},{3,12},{4,13},{5,14},{6,15},{7,16},{8,17},{9,1... | collective-permute-start | bytes 147464
  1369.2 66.3 %collective-permute-start.11 = (f32[8,1536]{1,0:T(8,128)S(1)}, f32[8,1536]{1,0:T(8,128)S(1)}, u32[]{:S(2)}, u32[]{:S(2)}) collective-permute-start(f32[8,1536]{1,0:T(8,128)S(1)} %fusion), channel_id=1, source_target_pairs={{0,8},{1,9},{2,10},{3,11},{4,12},{5,13},{6,14},{7,15},{8,16},{9,17... | collective-permute-start | bytes 147464
  1382.3 66.3 %collective-permute-start.10 = (f32[8,1536]{1,0:T(8,128)S(1)}, f32[8,1536]{1,0:T(8,128)S(1)}, u32[]{:S(2)}, u32[]{:S(2)}) collective-permute-start(f32[8,1536]{1,0:T(8,128)S(1)} %fusion), channel_id=1, source_target_pairs={{0,7},{1,8},{2,9},{3,10},{4,11},{5,12},{6,13},{7,14},{8,15},{9,16}... | collective-permute-start | bytes 147464
  1395.5 66.3 %collective-permute-start.9 = (f32[8,1536]{1,0:T(8,128)S(1)}, f32[8,1536]{1,0:T(8,128)S(1)}, u32[]{:S(2)}, u32[]{:S(2)}) collective-permute-start(f32[8,1536]{1,0:T(8,128)S(1)} %fusion), channel_id=1, source_target_pairs={{0,6},{1,7},{2,8},{3,9},{4,10},{5,11},{6,12},{7,13},{8,14},{9,15},... | collective-permute-start | bytes 147464
  1408.6 56.6 %collective-permute-start.8 = (f32[8,1536]{1,0:T(8,128)S(1)}, f32[8,1536]{1,0:T(8,128)}, u32[]{:S(2)}, u32[]{:S(2)}) collective-permute-start(f32[8,1536]{1,0:T(8,128)S(1)} %fusion), channel_id=1, source_target_pairs={{0,5},{1,6},{2,7},{3,8},{4,9},{5,10},{6,11},{7,12},{8,13},{9,14},{... | collective-permute-start | bytes 147464
  1422.4 42.8 %collective-permute-start.7 = (f32[8,1536]{1,0:T(8,128)S(1)}, f32[8,1536]{1,0:T(8,128)}, u32[]{:S(2)}, u32[]{:S(2)}) collective-permute-start(f32[8,1536]{1,0:T(8,128)S(1)} %fusion), channel_id=1, source_target_pairs={{0,4},{1,5},{2,6},{3,7},{4,8},{5,9},{6,10},{7,11},{8,12},{9,13},{1... | collective-permute-start | bytes 147464
  1435.5 29.7 %collective-permute-start.6 = (f32[8,1536]{1,0:T(8,128)S(1)}, f32[8,1536]{1,0:T(8,128)}, u32[]{:S(2)}, u32[]{:S(2)}) collective-permute-start(f32[8,1536]{1,0:T(8,128)S(1)} %fusion), channel_id=1, source_target_pairs={{0,3},{1,4},{2,5},{3,6},{4,7},{5,8},{6,9},{7,10},{8,11},{9,12},{10... | collective-permute-start | bytes 147464
  1448.7 16.5 collective-permute-start.5
  1667.3 10.8 collective-permute-start.2
  1669.9 8.2 collective-permute-start.3
  (94 other events, 10894.2 us)
Sparse Core Ops, SparseCore 0:
  11.9 120.5 all-gather.3
  1678.2 246.9 all-reduce.7
where the time goes:
time: 1950 us; the launch traced here: 1930 us
  blocking collectives  1010 us (52%)
  starting transfers between devices  502 us (26%)
  waiting for transfers between devices  239 us (12%)
  local copies, waits for them, and re-layouts  129 us (7%)
  other arithmetic  27.6 us (1%)
    unnamed x1, blocking collectives  710 us
    unnamed x65, starting transfers between devices  489 us
    unnamed x67, waiting for transfers between devices  239 us
    unnamed x183, local copies, waits for them, and re-layouts  109 us
    psum x1, blocking collectives, local(): lax.psum((jnp.sum(grad_pre * normed, axis=0), jnp.sum(grad_pre, axis=0)),...  79.5 us
    psum x1, blocking collectives, local(): lax.psum((jnp.sum(weight_col * conv, axis=0), jnp.sum(weight_col)), ('dp'...  75.7 us
    psum x1, blocking collectives, local(): lax.psum(jnp.sum(weight_col * centred * centred, axis=0), ('dp', 'pair'))  74.2 us
    all_gather x1, blocking collectives, local(): params_full = lax.all_gather(stacked, ('dp', 'pair'), axis=1, tiled=True)  68 us
  transfers between devices with their start and end apart: 70, of which 3 were waited for; matrix products, arithmetic and copies ran while one was open for 44% of the time, Pallas kernels for 0%

commit v1 on v0

--- a/solution.py
+++ b/solution.py
@@ -52,7 +52,9 @@
     )
     mean = total / count
     centred = conv - mean
-    spread = lax.psum(jnp.sum(weight_col * centred * centred, axis=0), ("dp", "pair"))
+    spread = jnp.sum(
+        lax.all_gather(jnp.sum(weight_col * centred * centred, axis=0), ("dp", "pair")), axis=0
+    )
     variance = spread / count
     inv_std = lax.rsqrt(variance + 1e-05)
     normed = centred * inv_std

time: 1950 us -> 1980 us (1.015)
  waiting for transfers between devices: 239 us -> 338 us
  blocking collectives: 1010 us -> 937 us
    all_gather x0 -> x1, waiting for transfers between devices: none -> 99.4 us  [local(): lax.all_gather(jnp.sum(weight_col * centred * centred, axis=0), ('dp', 'p...]
    psum x1 -> x0, blocking collectives: 74.2 us -> none  [local(): lax.psum(jnp.sum(weight_col * centred * centred, axis=0), ('dp', 'pair'))]
    unnamed x183 -> x184, local copies, waits for them, and re-layouts: 109 us -> 110 us
    unnamed x67 -> x68, waiting for transfers between devices: 239 us -> 239 us
  transfers between devices with their start and end apart: 70 -> 71, of which waited for: 3 -> 3; matrix products, arithmetic and copies ran while one was open for 44% -> 43% of each run, Pallas kernels for 0% -> 0%
where the time goes in v1:
time: 1980 us; the launch traced here: 1960 us
  blocking collectives  937 us (47%)
  starting transfers between devices  501 us (25%)
  waiting for transfers between devices  338 us (17%)
  local copies, waits for them, and re-layouts  130 us (7%)
  other arithmetic  29.9 us (2%)
    unnamed x1, blocking collectives  714 us
    unnamed x65, starting transfers between devices  489 us
    unnamed x68, waiting for transfers between devices  239 us
    unnamed x184, local copies, waits for them, and re-layouts  110 us
    all_gather x1, waiting for transfers between devices, local(): lax.all_gather(jnp.sum(weight_col * centred * centred, axis=0), ('dp', 'p...  99.4 us
    psum x1, blocking collectives, local(): lax.psum((jnp.sum(grad_pre * normed, axis=0), jnp.sum(grad_pre, axis=0)),...  79.5 us
    psum x1, blocking collectives, local(): lax.psum((jnp.sum(weight_col * conv, axis=0), jnp.sum(weight_col)), ('dp'...  75 us
    all_gather x1, blocking collectives, local(): params_full = lax.all_gather(stacked, ('dp', 'pair'), axis=1, tiled=True)  67.9 us
  transfers between devices with their start and end apart: 71, of which 3 were waited for; matrix products, arithmetic and copies ran while one was open for 43% of the time, Pallas kernels for 0%

profile of v1, /device:TPU:1, one launch (start us, length us, event | category | flops | bytes accessed | tf_op | source)
XLA Modules:
  0.0 1964.8 jit_solution(13123529041177388765)
XLA Ops:
  9.0 4.6 collective-permute-start
  13.7 1.9 collective-permute-start.1
  19.2 67.9 %all-gather.1 = f32[256,6,33]{2,1,0:T(8,128)S(1)} all-gather(f32[1,6,33]{2,1,0:T(8,128)S(1)} %maximum_bitcast_fusion), channel_id=1, replica_groups=mesh['dp'=128,'pair'=2] {'dp','pair'}, dimensions={0}, use_global_device_ids=true | all-gather | bytes 203544 | tf_op jit(solution)/shard_map/all_gather | solution.py:35
  87.2 5.6 slice_reduce_fusion.31
  92.8 8.2 slice_reduce_fusion.32
  102.0 4.6 multiply_reduce_fusion.2
  106.6 75.0 %all-reduce.5 = (f32[1536]{0:T(1024)S(1)}, f32[]{:T(128)}) all-reduce(f32[1536]{0:T(1024)S(1)} %get-tuple-element.89, f32[]{:T(128)} %convert_reduce_fusion), channel_id=1, replica_groups=mesh['dp'=128,'pair'=2] {'dp','pair'}, use_global_device_ids=true, to_apply=%region_1.2 | all-reduce | flops 1537 | bytes 12296 | tf_op jit(solution)/shard_map/psum | solution.py:50
  183.9 99.4 %all-gather.7.cloned.1.call-done = f32[256,1,1536]{2,1,0:T(1,128)} async-done(((f32[1,1,1536]{2,1,0:T(1,128)}), f32[256,1,1536]{2,1,0:T(1,128)}) %all-gather.7.cloned.1.call-update) | async-done | bytes 1572880 | tf_op jit(solution)/shard_map/all_gather | solution.py:56
  283.3 2.3 reduce_sum.336
  286.3 5.2 fusion.124
  291.5 714.2 %fusion = f32[8,1536]{1,0:T(8,128)S(1)} fusion(f32[1536,1536]{1,0:T(8,128)} %fusion.124), kind=kCustom, calls=%all-reduce-scatter | all-reduce-scatter fusion | flops 3145729 | bytes 9486336
  1010.2 11.0 collective-permute-start.67
  1037.0 17.9 collective-permute-start.51
  1054.9 3.1 collective-permute-start.50
  1059.7 3.1 collective-permute-start.48
  1062.8 3.9 collective-permute-start.47
  1066.7 3.9 collective-permute-start.46
  1077.2 2.8 collective-permute-start.40
  1080.1 3.3 collective-permute-start.39
  1083.4 2.5 collective-permute-start.38
  1085.9 4.3 collective-permute-start.37
  1091.8 6.1 collective-permute-start.35
  1098.0 13.1 collective-permute-start.34
  1111.1 13.1 collective-permute-start.33
  1124.3 13.1 collective-permute-start.32
  1137.4 13.1 collective-permute-start.31
  1150.6 13.1 collective-permute-start.30
  1163.7 13.1 collective-permute-start.29
  1176.9 13.1 collective-permute-start.28
  1190.0 13.1 collective-permute-start.27
  1203.2 13.1 collective-permute-start.26
  1216.3 13.1 collective-permute-start.25
  1229.5 13.1 collective-permute-start.24
  1242.6 13.1 collective-permute-start.23
  1255.8 13.1 collective-permute-start.22
  1268.9 13.1 collective-permute-start.21
  1282.1 13.1 collective-permute-start.20
  1295.2 13.1 collective-permute-start.19
  1308.4 13.1 collective-permute-start.18
  1321.5 13.1 collective-permute-start.17
  1334.7 13.1 collective-permute-start.16
  1347.8 13.3 collective-permute-start.15
  1361.1 13.1 collective-permute-start.14
  1374.3 13.1 collective-permute-start.13
  1387.4 13.1 collective-permute-start.12
  1400.6 13.1 collective-permute-start.11
  1413.7 13.1 collective-permute-start.10
  1426.9 13.1 collective-permute-start.9
  1440.0 13.7 collective-permute-start.8
  1453.8 13.1 collective-permute-start.7
  1466.9 13.1 collective-permute-start.6
  1480.1 13.1 collective-permute-start.5
  1493.2 3.0 collective-permute-start.4
  1497.4 97.2 %concatenate.45 = f32[518,1536]{1,0:T(8,128)} concatenate(f32[6,1536]{1,0:T(8,128)S(1)} %collective-permute-done.67, f32[8,1536]{1,0:T(8,128)S(1)} %collective-permute-done.66, f32[8,1536]{1,0:T(8,128)S(1)} %collective-permute-done.65, f32[8,1536]{1,0:T(8,128)S(1)} %collective-permute-done.64, f32[8,1536]{1,0:T(8,128)S(1)} %collective-permute-done.63, ...), dimensions={0} | concatenate | bytes 6365184
  1596.1 8.4 reshape.59
  1604.5 4.1 convolution_convert_fusion
  1608.7 2.6 fusion.125
  1611.4 79.5 %all-reduce.4 = (f32[1536]{0:T(1024)S(1)}, f32[1536]{0:T(1024)S(1)}) all-reduce(f32[1536]{0:T(1024)S(1)} %get-tuple-element.50, f32[1536]{0:T(1024)S(1)} %get-tuple-element.49), channel_id=1, replica_groups=mesh['dp'=128,'pair'=2] {'dp','pair'}, use_global_device_ids=true, to_apply=%region_9.10 | all-reduce | flops 3072 | bytes 24576 | tf_op jit(solution)/shard_map/psum | solution.py:70
  1691.7 3.5 select_reduce_fusion
  1698.7 2.6 collective-permute-start.2
  1701.3 3.2 collective-permute-start.3
  1706.7 2.7 stack.127
  1709.5 9.9 fusion.9
  1719.4 237.1 %all-reduce.8.cloned.1.call-done = f32[31,1536]{1,0:T(8,128)} async-done(((f32[31,1536]{1,0:T(8,128)}), f32[31,1536]{1,0:T(8,128)}) %all-reduce.8.cloned.1.call-update) | async-done | bytes 190480
  (334 shorter events, 48.7 us)
Async XLA Ops:
  7.2 276.1 %all-gather.7.cloned.1.call-start = ((), (), s32[]{:S(2)}) async-start(), calls=%async_computation | async-start | bytes 1579008 | tf_op jit(solution)/shard_map/all_gather | solution.py:56
  9.0 92.6 %collective-permute-start = (bf16[15,1536]{1,0:T(8,128)(2,1)S(1)}, bf16[15,1536]{1,0:T(8,128)(2,1)S(1)}, u32[]{:S(2)}, u32[]{:S(2)}) collective-permute-start(bf16[15,1536]{1,0:T(8,128)(2,1)S(1)} %get-tuple-element.93), channel_id=1, source_target_pairs={{0,1},{1,2},{2,3},{3,4},{4,5},{5,6},{6,7},{7,8},{8,9},{9,10},{10,1... | collective-permute-start | bytes 138248 | tf_op jit(solution)/shard_map/ppermute | solution.py:17
  13.7 88.0 %collective-permute-start.1 = (bf16[15,1536]{1,0:T(8,128)(2,1)S(1)}, bf16[15,1536]{1,0:T(8,128)(2,1)S(1)}, u32[]{:S(2)}, u32[]{:S(2)}) collective-permute-start(bf16[15,1536]{1,0:T(8,128)(2,1)S(1)} %get-tuple-element.94), channel_id=1, source_target_pairs={{1,0},{2,1},{3,2},{4,3},{5,4},{6,5},{7,6},{8,7},{9,8},{10,9},{11,1... | collective-permute-start | bytes 138248 | tf_op jit(solution)/shard_map/ppermute | solution.py:19
  183.1 1413.1 %all-gather.9.cloned.1.call-start = ((), (), s32[]{:S(2)}) async-start(), calls=%async_computation.1 | async-start | bytes 6316032 | tf_op jit(solution)/shard_map/all_gather | solution.py:64
  183.8 1772.7 %all-reduce.8.cloned.1.call-start = ((), (), s32[]{:S(2)}) async-start(), calls=%async_computation.2 | async-start | bytes 393216
  1005.7 18.2 collective-permute-start.66
  1007.0 18.2 collective-permute-start.65
  1008.9 17.6 collective-permute-start.64
  1010.2 12.3 collective-permute-start.67
  1021.2 6.5 collective-permute-start.63
  1022.6 6.5 collective-permute-start.62
  1031.7 23.2 %collective-permute-start.55 = (f32[8,1536]{1,0:T(8,128)S(1)}, f32[8,1536]{1,0:T(8,128)S(1)}, u32[]{:S(2)}, u32[]{:S(2)}) collective-permute-start(f32[8,1536]{1,0:T(8,128)S(1)} %fusion), channel_id=1, source_target_pairs={{0,52},{1,53},{2,54},{3,55},{4,56},{5,57},{6,58},{7,59},{8,60},{9,... | collective-permute-start | bytes 147464
  1033.0 25.0 %collective-permute-start.54 = (f32[8,1536]{1,0:T(8,128)S(1)}, f32[8,1536]{1,0:T(8,128)S(1)}, u32[]{:S(2)}, u32[]{:S(2)}) collective-permute-start(f32[8,1536]{1,0:T(8,128)S(1)} %fusion), channel_id=1, source_target_pairs={{0,51},{1,52},{2,53},{3,54},{4,55},{5,56},{6,57},{7,58},{8,59},{9,... | collective-permute-start | bytes 147464
  1034.3 25.3 %collective-permute-start.53 = (f32[8,1536]{1,0:T(8,128)S(1)}, f32[8,1536]{1,0:T(8,128)S(1)}, u32[]{:S(2)}, u32[]{:S(2)}) collective-permute-start(f32[8,1536]{1,0:T(8,128)S(1)} %fusion), channel_id=1, source_target_pairs={{0,50},{1,51},{2,52},{3,53},{4,54},{5,55},{6,56},{7,57},{8,58},{9,... | collective-permute-start | bytes 147464
  1035.7 27.1 %collective-permute-start.52 = (f32[8,1536]{1,0:T(8,128)S(1)}, f32[8,1536]{1,0:T(8,128)S(1)}, u32[]{:S(2)}, u32[]{:S(2)}) collective-permute-start(f32[8,1536]{1,0:T(8,128)S(1)} %fusion), channel_id=1, source_target_pairs={{0,49},{1,50},{2,51},{3,52},{4,53},{5,54},{6,55},{7,56},{8,57},{9,... | collective-permute-start | bytes 147464
  1037.0 29.7 %collective-permute-start.51 = (f32[8,1536]{1,0:T(8,128)S(1)}, f32[8,1536]{1,0:T(8,128)S(1)}, u32[]{:S(2)}, u32[]{:S(2)}) collective-permute-start(f32[8,1536]{1,0:T(8,128)S(1)} %fusion), channel_id=1, source_target_pairs={{0,48},{1,49},{2,50},{3,51},{4,52},{5,53},{6,54},{7,55},{8,56},{9,... | collective-permute-start | bytes 147464
  1054.9 15.7 collective-permute-start.50
  1058.0 13.9 collective-permute-start.49
  1059.7 13.6 collective-permute-start.48
  1062.8 11.8 collective-permute-start.47
  1066.7 9.2 collective-permute-start.46
  1070.6 6.6 collective-permute-start.45
  1071.9 8.1 collective-permute-start.44
  1073.3 10.1 collective-permute-start.43
  1074.6 11.3 collective-permute-start.42
  1075.9 14.3 collective-permute-start.41
  1077.2 14.6 collective-permute-start.40
  1080.1 17.9 collective-permute-start.39
  1083.4 27.7 %collective-permute-start.38 = (f32[8,1536]{1,0:T(8,128)S(1)}, f32[8,1536]{1,0:T(8,128)S(1)}, u32[]{:S(2)}, u32[]{:S(2)}) collective-permute-start(f32[8,1536]{1,0:T(8,128)S(1)} %fusion), channel_id=1, source_target_pairs={{0,35},{1,36},{2,37},{3,38},{4,39},{5,40},{6,41},{7,42},{8,43},{9,... | collective-permute-start | bytes 147464
  1085.9 38.4 %collective-permute-start.37 = (f32[8,1536]{1,0:T(8,128)S(1)}, f32[8,1536]{1,0:T(8,128)S(1)}, u32[]{:S(2)}, u32[]{:S(2)}) collective-permute-start(f32[8,1536]{1,0:T(8,128)S(1)} %fusion), channel_id=1, source_target_pairs={{0,34},{1,35},{2,36},{3,37},{4,38},{5,39},{6,40},{7,41},{8,42},{9,... | collective-permute-start | bytes 147464
  1090.2 47.2 %collective-permute-start.36 = (f32[8,1536]{1,0:T(8,128)S(1)}, f32[8,1536]{1,0:T(8,128)S(1)}, u32[]{:S(2)}, u32[]{:S(2)}) collective-permute-start(f32[8,1536]{1,0:T(8,128)S(1)} %fusion), channel_id=1, source_target_pairs={{0,33},{1,34},{2,35},{3,36},{4,37},{5,38},{6,39},{7,40},{8,41},{9,... | collective-permute-start | bytes 147464
  1091.8 58.7 %collective-permute-start.35 = (f32[8,1536]{1,0:T(8,128)S(1)}, f32[8,1536]{1,0:T(8,128)S(1)}, u32[]{:S(2)}, u32[]{:S(2)}) collective-permute-start(f32[8,1536]{1,0:T(8,128)S(1)} %fusion), channel_id=1, source_target_pairs={{0,32},{1,33},{2,34},{3,35},{4,36},{5,37},{6,38},{7,39},{8,40},{9,... | collective-permute-start | bytes 147464
  1098.0 65.7 %collective-permute-start.34 = (f32[8,1536]{1,0:T(8,128)S(1)}, f32[8,1536]{1,0:T(8,128)S(1)}, u32[]{:S(2)}, u32[]{:S(2)}) collective-permute-start(f32[8,1536]{1,0:T(8,128)S(1)} %fusion), channel_id=1, source_target_pairs={{0,31},{1,32},{2,33},{3,34},{4,35},{5,36},{6,37},{7,38},{8,39},{9,... | collective-permute-start | bytes 147464
  1111.1 65.7 %collective-permute-start.33 = (f32[8,1536]{1,0:T(8,128)S(1)}, f32[8,1536]{1,0:T(8,128)S(1)}, u32[]{:S(2)}, u32[]{:S(2)}) collective-permute-start(f32[8,1536]{1,0:T(8,128)S(1)} %fusion), channel_id=1, source_target_pairs={{0,30},{1,31},{2,32},{3,33},{4,34},{5,35},{6,36},{7,37},{8,38},{9,... | collective-permute-start | bytes 147464
  1124.3 65.7 %collective-permute-start.32 = (f32[8,1536]{1,0:T(8,128)S(1)}, f32[8,1536]{1,0:T(8,128)S(1)}, u32[]{:S(2)}, u32[]{:S(2)}) collective-permute-start(f32[8,1536]{1,0:T(8,128)S(1)} %fusion), channel_id=1, source_target_pairs={{0,29},{1,30},{2,31},{3,32},{4,33},{5,34},{6,35},{7,36},{8,37},{9,... | collective-permute-start | bytes 147464
  1137.4 65.7 %collective-permute-start.31 = (f32[8,1536]{1,0:T(8,128)S(1)}, f32[8,1536]{1,0:T(8,128)S(1)}, u32[]{:S(2)}, u32[]{:S(2)}) collective-permute-start(f32[8,1536]{1,0:T(8,128)S(1)} %fusion), channel_id=1, source_target_pairs={{0,28},{1,29},{2,30},{3,31},{4,32},{5,33},{6,34},{7,35},{8,36},{9,... | collective-permute-start | bytes 147464
  1150.6 65.7 %collective-permute-start.30 = (f32[8,1536]{1,0:T(8,128)S(1)}, f32[8,1536]{1,0:T(8,128)S(1)}, u32[]{:S(2)}, u32[]{:S(2)}) collective-permute-start(f32[8,1536]{1,0:T(8,128)S(1)} %fusion), channel_id=1, source_target_pairs={{0,27},{1,28},{2,29},{3,30},{4,31},{5,32},{6,33},{7,34},{8,35},{9,... | collective-permute-start | bytes 147464
  1163.7 65.7 %collective-permute-start.29 = (f32[8,1536]{1,0:T(8,128)S(1)}, f32[8,1536]{1,0:T(8,128)S(1)}, u32[]{:S(2)}, u32[]{:S(2)}) collective-permute-start(f32[8,1536]{1,0:T(8,128)S(1)} %fusion), channel_id=1, source_target_pairs={{0,26},{1,27},{2,28},{3,29},{4,30},{5,31},{6,32},{7,33},{8,34},{9,... | collective-permute-start | bytes 147464
  1176.9 65.7 %collective-permute-start.28 = (f32[8,1536]{1,0:T(8,128)S(1)}, f32[8,1536]{1,0:T(8,128)S(1)}, u32[]{:S(2)}, u32[]{:S(2)}) collective-permute-start(f32[8,1536]{1,0:T(8,128)S(1)} %fusion), channel_id=1, source_target_pairs={{0,25},{1,26},{2,27},{3,28},{4,29},{5,30},{6,31},{7,32},{8,33},{9,... | collective-permute-start | bytes 147464
  1190.0 65.7 %collective-permute-start.27 = (f32[8,1536]{1,0:T(8,128)S(1)}, f32[8,1536]{1,0:T(8,128)S(1)}, u32[]{:S(2)}, u32[]{:S(2)}) collective-permute-start(f32[8,1536]{1,0:T(8,128)S(1)} %fusion), channel_id=1, source_target_pairs={{0,24},{1,25},{2,26},{3,27},{4,28},{5,29},{6,30},{7,31},{8,32},{9,... | collective-permute-start | bytes 147464
  1203.2 65.7 %collective-permute-start.26 = (f32[8,1536]{1,0:T(8,128)S(1)}, f32[8,1536]{1,0:T(8,128)S(1)}, u32[]{:S(2)}, u32[]{:S(2)}) collective-permute-start(f32[8,1536]{1,0:T(8,128)S(1)} %fusion), channel_id=1, source_target_pairs={{0,23},{1,24},{2,25},{3,26},{4,27},{5,28},{6,29},{7,30},{8,31},{9,... | collective-permute-start | bytes 147464
  1216.3 65.7 %collective-permute-start.25 = (f32[8,1536]{1,0:T(8,128)S(1)}, f32[8,1536]{1,0:T(8,128)S(1)}, u32[]{:S(2)}, u32[]{:S(2)}) collective-permute-start(f32[8,1536]{1,0:T(8,128)S(1)} %fusion), channel_id=1, source_target_pairs={{0,22},{1,23},{2,24},{3,25},{4,26},{5,27},{6,28},{7,29},{8,30},{9,... | collective-permute-start | bytes 147464
  1229.5 65.7 %collective-permute-start.24 = (f32[8,1536]{1,0:T(8,128)S(1)}, f32[8,1536]{1,0:T(8,128)S(1)}, u32[]{:S(2)}, u32[]{:S(2)}) collective-permute-start(f32[8,1536]{1,0:T(8,128)S(1)} %fusion), channel_id=1, source_target_pairs={{0,21},{1,22},{2,23},{3,24},{4,25},{5,26},{6,27},{7,28},{8,29},{9,... | collective-permute-start | bytes 147464
  1242.6 65.7 %collective-permute-start.23 = (f32[8,1536]{1,0:T(8,128)S(1)}, f32[8,1536]{1,0:T(8,128)S(1)}, u32[]{:S(2)}, u32[]{:S(2)}) collective-permute-start(f32[8,1536]{1,0:T(8,128)S(1)} %fusion), channel_id=1, source_target_pairs={{0,20},{1,21},{2,22},{3,23},{4,24},{5,25},{6,26},{7,27},{8,28},{9,... | collective-permute-start | bytes 147464
  1255.8 65.7 %collective-permute-start.22 = (f32[8,1536]{1,0:T(8,128)S(1)}, f32[8,1536]{1,0:T(8,128)S(1)}, u32[]{:S(2)}, u32[]{:S(2)}) collective-permute-start(f32[8,1536]{1,0:T(8,128)S(1)} %fusion), channel_id=1, source_target_pairs={{0,19},{1,20},{2,21},{3,22},{4,23},{5,24},{6,25},{7,26},{8,27},{9,... | collective-permute-start | bytes 147464
  1268.9 65.7 %collective-permute-start.21 = (f32[8,1536]{1,0:T(8,128)S(1)}, f32[8,1536]{1,0:T(8,128)S(1)}, u32[]{:S(2)}, u32[]{:S(2)}) collective-permute-start(f32[8,1536]{1,0:T(8,128)S(1)} %fusion), channel_id=1, source_target_pairs={{0,18},{1,19},{2,20},{3,21},{4,22},{5,23},{6,24},{7,25},{8,26},{9,... | collective-permute-start | bytes 147464
  1282.1 65.7 %collective-permute-start.20 = (f32[8,1536]{1,0:T(8,128)S(1)}, f32[8,1536]{1,0:T(8,128)S(1)}, u32[]{:S(2)}, u32[]{:S(2)}) collective-permute-start(f32[8,1536]{1,0:T(8,128)S(1)} %fusion), channel_id=1, source_target_pairs={{0,17},{1,18},{2,19},{3,20},{4,21},{5,22},{6,23},{7,24},{8,25},{9,... | collective-permute-start | bytes 147464
  1295.2 65.9 %collective-permute-start.19 = (f32[8,1536]{1,0:T(8,128)S(1)}, f32[8,1536]{1,0:T(8,128)S(1)}, u32[]{:S(2)}, u32[]{:S(2)}) collective-permute-start(f32[8,1536]{1,0:T(8,128)S(1)} %fusion), channel_id=1, source_target_pairs={{0,16},{1,17},{2,18},{3,19},{4,20},{5,21},{6,22},{7,23},{8,24},{9,... | collective-permute-start | bytes 147464
  1308.4 65.9 %collective-permute-start.18 = (f32[8,1536]{1,0:T(8,128)S(1)}, f32[8,1536]{1,0:T(8,128)S(1)}, u32[]{:S(2)}, u32[]{:S(2)}) collective-permute-start(f32[8,1536]{1,0:T(8,128)S(1)} %fusion), channel_id=1, source_target_pairs={{0,15},{1,16},{2,17},{3,18},{4,19},{5,20},{6,21},{7,22},{8,23},{9,... | collective-permute-start | bytes 147464
  1321.5 65.9 %collective-permute-start.17 = (f32[8,1536]{1,0:T(8,128)S(1)}, f32[8,1536]{1,0:T(8,128)S(1)}, u32[]{:S(2)}, u32[]{:S(2)}) collective-permute-start(f32[8,1536]{1,0:T(8,128)S(1)} %fusion), channel_id=1, source_target_pairs={{0,14},{1,15},{2,16},{3,17},{4,18},{5,19},{6,20},{7,21},{8,22},{9,... | collective-permute-start | bytes 147464
  1334.7 65.9 %collective-permute-start.16 = (f32[8,1536]{1,0:T(8,128)S(1)}, f32[8,1536]{1,0:T(8,128)S(1)}, u32[]{:S(2)}, u32[]{:S(2)}) collective-permute-start(f32[8,1536]{1,0:T(8,128)S(1)} %fusion), channel_id=1, source_target_pairs={{0,13},{1,14},{2,15},{3,16},{4,17},{5,18},{6,19},{7,20},{8,21},{9,... | collective-permute-start | bytes 147464
  1347.8 65.9 %collective-permute-start.15 = (f32[8,1536]{1,0:T(8,128)S(1)}, f32[8,1536]{1,0:T(8,128)S(1)}, u32[]{:S(2)}, u32[]{:S(2)}) collective-permute-start(f32[8,1536]{1,0:T(8,128)S(1)} %fusion), channel_id=1, source_target_pairs={{0,12},{1,13},{2,14},{3,15},{4,16},{5,17},{6,18},{7,19},{8,20},{9,... | collective-permute-start | bytes 147464
  1361.1 65.7 %collective-permute-start.14 = (f32[8,1536]{1,0:T(8,128)S(1)}, f32[8,1536]{1,0:T(8,128)S(1)}, u32[]{:S(2)}, u32[]{:S(2)}) collective-permute-start(f32[8,1536]{1,0:T(8,128)S(1)} %fusion), channel_id=1, source_target_pairs={{0,11},{1,12},{2,13},{3,14},{4,15},{5,16},{6,17},{7,18},{8,19},{9,... | collective-permute-start | bytes 147464
  1374.3 65.7 %collective-permute-start.13 = (f32[8,1536]{1,0:T(8,128)S(1)}, f32[8,1536]{1,0:T(8,128)S(1)}, u32[]{:S(2)}, u32[]{:S(2)}) collective-permute-start(f32[8,1536]{1,0:T(8,128)S(1)} %fusion), channel_id=1, source_target_pairs={{0,10},{1,11},{2,12},{3,13},{4,14},{5,15},{6,16},{7,17},{8,18},{9,... | collective-permute-start | bytes 147464
  1387.4 66.3 %collective-permute-start.12 = (f32[8,1536]{1,0:T(8,128)S(1)}, f32[8,1536]{1,0:T(8,128)S(1)}, u32[]{:S(2)}, u32[]{:S(2)}) collective-permute-start(f32[8,1536]{1,0:T(8,128)S(1)} %fusion), channel_id=1, source_target_pairs={{0,9},{1,10},{2,11},{3,12},{4,13},{5,14},{6,15},{7,16},{8,17},{9,1... | collective-permute-start | bytes 147464
  1400.6 66.3 %collective-permute-start.11 = (f32[8,1536]{1,0:T(8,128)S(1)}, f32[8,1536]{1,0:T(8,128)S(1)}, u32[]{:S(2)}, u32[]{:S(2)}) collective-permute-start(f32[8,1536]{1,0:T(8,128)S(1)} %fusion), channel_id=1, source_target_pairs={{0,8},{1,9},{2,10},{3,11},{4,12},{5,13},{6,14},{7,15},{8,16},{9,17... | collective-permute-start | bytes 147464
  1413.7 66.3 %collective-permute-start.10 = (f32[8,1536]{1,0:T(8,128)S(1)}, f32[8,1536]{1,0:T(8,128)S(1)}, u32[]{:S(2)}, u32[]{:S(2)}) collective-permute-start(f32[8,1536]{1,0:T(8,128)S(1)} %fusion), channel_id=1, source_target_pairs={{0,7},{1,8},{2,9},{3,10},{4,11},{5,12},{6,13},{7,14},{8,15},{9,16}... | collective-permute-start | bytes 147464
  1426.9 66.3 %collective-permute-start.9 = (f32[8,1536]{1,0:T(8,128)S(1)}, f32[8,1536]{1,0:T(8,128)S(1)}, u32[]{:S(2)}, u32[]{:S(2)}) collective-permute-start(f32[8,1536]{1,0:T(8,128)S(1)} %fusion), channel_id=1, source_target_pairs={{0,6},{1,7},{2,8},{3,9},{4,10},{5,11},{6,12},{7,13},{8,14},{9,15},... | collective-permute-start | bytes 147464
  1440.0 56.6 %collective-permute-start.8 = (f32[8,1536]{1,0:T(8,128)S(1)}, f32[8,1536]{1,0:T(8,128)}, u32[]{:S(2)}, u32[]{:S(2)}) collective-permute-start(f32[8,1536]{1,0:T(8,128)S(1)} %fusion), channel_id=1, source_target_pairs={{0,5},{1,6},{2,7},{3,8},{4,9},{5,10},{6,11},{7,12},{8,13},{9,14},{... | collective-permute-start | bytes 147464
  1453.8 42.8 %collective-permute-start.7 = (f32[8,1536]{1,0:T(8,128)S(1)}, f32[8,1536]{1,0:T(8,128)}, u32[]{:S(2)}, u32[]{:S(2)}) collective-permute-start(f32[8,1536]{1,0:T(8,128)S(1)} %fusion), channel_id=1, source_target_pairs={{0,4},{1,5},{2,6},{3,7},{4,8},{5,9},{6,10},{7,11},{8,12},{9,13},{1... | collective-permute-start | bytes 147464
  1466.9 29.7 %collective-permute-start.6 = (f32[8,1536]{1,0:T(8,128)S(1)}, f32[8,1536]{1,0:T(8,128)}, u32[]{:S(2)}, u32[]{:S(2)}) collective-permute-start(f32[8,1536]{1,0:T(8,128)S(1)} %fusion), channel_id=1, source_target_pairs={{0,3},{1,4},{2,5},{3,6},{4,7},{5,8},{6,9},{7,10},{8,11},{9,12},{10... | collective-permute-start | bytes 147464
  1480.1 16.5 collective-permute-start.5
  1698.7 10.8 collective-permute-start.2
  1701.3 8.2 collective-permute-start.3
  (95 other events, 12544.5 us)
Sparse Core Ops, SparseCore 0:
  183.2 100.0 all-gather.6
  287.2 115.8 all-gather.8
  1709.6 246.9 all-reduce.7
